TPU v7x, 32 devices: a whole 2x2x4 slice. The times are simulated.
32 devices in a mesh: parts: 2 (over x), row: 4 (over y, core), col: 4 (over z).
Axes of the slice: x: 2, y: 2, z: 4, core: 2. Of those that a mesh axis runs over, the one named last changes fastest.
Arguments:
- pair: bfloat16 [192, 96, 128], P(('parts', 'row'), 'col'), parts along dimension 0, may hold values from -6 to 6
- residue_count: int32 [2], P('parts'), parts along dimension 0, may hold values from 48 to 96
- out_norm: float32 [128], replicated, may hold values from 0.1 to 1.9
- out_proj: bfloat16 [128, 512], replicated, may hold values from -0.5 to 0.5
- out_gate: bfloat16 [128, 128], replicated, may hold values from -0.5 to 0.5
- out_mix_norm: float32 [128], replicated, may hold values from 0.1 to 1.9
- out_final: bfloat16 [128, 128], replicated, may hold values from -0.5 to 0.5
- inc_norm: float32 [128], replicated, may hold values from 0.1 to 1.9
- inc_proj: bfloat16 [128, 512], replicated, may hold values from -0.5 to 0.5
- inc_gate: bfloat16 [128, 128], replicated, may hold values from -0.5 to 0.5
- inc_mix_norm: float32 [128], replicated, may hold values from 0.1 to 1.9
- inc_final: bfloat16 [128, 128], replicated, may hold values from -0.5 to 0.5
- transition_norm: float32 [128], replicated, may hold values from 0.1 to 1.9
- transition_up: bfloat16 [128, 1024], replicated, may hold values from -0.5 to 0.5
- transition_down: bfloat16 [512, 128], replicated, may hold values from -0.25 to 0.25
Outputs:
- result: bfloat16 [192, 96, 128], P(('parts', 'row'), 'col'), parts along dimension 0
There are 2 independent parts, one for each index of `parts`. A program takes and returns all parts, laid end to end along the dimension named above; an argument that names none is the same for every part. Nothing has to cross between parts.
Inputs may be any that keep to these rules, and one draw needn't show every extreme that they name: `residue_count`: how many residues of the complex are real; positions below it are real, the others padding.
All inputs are finite; a program needn't handle non-finite values.
Results may differ from a plain program's by a relative error of at most 0.015.
Values may be sent and summed in bfloat16 or wider, within the bound.
A program may use at most 128 MiB of HBM per device.

v0:
```python
import jax
import jax.numpy as jnp
from jax import lax
from jax.sharding import PartitionSpec as P


def layer_norm(values, gain, axis):
    mean = jnp.mean(values, axis=axis, keepdims=True)
    centred = values - mean
    spread = jnp.mean(centred * centred, axis=axis, keepdims=True)
    return centred * lax.rsqrt(spread + 1e-05) * gain


def project(current, norm_gain, proj_w, gate_w, mask, form):
    normed = layer_norm(current.astype(jnp.float32), norm_gain, -1).astype(jnp.bfloat16)
    hidden = proj_w.shape[1] // 4
    left_part = jnp.einsum(
        form, normed, proj_w[:, : 2 * hidden], preferred_element_type=jnp.float32
    )
    left = (mask * jax.nn.sigmoid(left_part[:hidden]) * left_part[hidden:]).astype(jnp.bfloat16)
    right_part = jnp.einsum(
        form, normed, proj_w[:, 2 * hidden :], preferred_element_type=jnp.float32
    )
    right = (mask * jax.nn.sigmoid(right_part[:hidden]) * right_part[hidden:]).astype(jnp.bfloat16)
    gate = jnp.einsum("ijc,cd->ijd", normed, gate_w, preferred_element_type=jnp.float32)
    return (left, right, gate)


def finish(current, mixed, mix_gain, final_w, gate, form):
    mixnormed = layer_norm(mixed.astype(jnp.float32), mix_gain[:, None, None], 0).astype(
        jnp.bfloat16
    )
    change = jnp.einsum(form, mixnormed, final_w, preferred_element_type=jnp.float32)
    return (current.astype(jnp.float32) + jax.nn.sigmoid(gate) * change).astype(jnp.bfloat16)


def mix_over_col(left, right, incoming):
    left_wide, right_wide = (
        lax.all_to_all(left, "col", split_axis=0, concat_axis=2, tiled=True),
        lax.all_to_all(right, "col", split_axis=0, concat_axis=2, tiled=True),
    )
    if incoming:
        left_swapped = lax.all_to_all(left_wide, "row", split_axis=2, concat_axis=1, tiled=True)
        mixed = jnp.einsum(
            "hki,hkj->hij",
            left_swapped,
            lax.all_gather(right_wide, "row", axis=1, tiled=True),
            preferred_element_type=jnp.float32,
        )
    else:
        mixed = jnp.einsum(
            "hik,hjk->hij",
            left_wide,
            lax.all_gather(right_wide, "row", axis=1, tiled=True),
            preferred_element_type=jnp.float32,
        )
    return lax.all_to_all(
        mixed.astype(jnp.bfloat16), "col", split_axis=2, concat_axis=0, tiled=True
    )


def triangle(current, norm_gain, proj_w, gate_w, mix_gain, final_w, mask, incoming):
    left, right, gate = project(current, norm_gain, proj_w, gate_w, mask, "ijc,cf->fij")
    mixed = mix_over_col(left, right, incoming)
    return finish(current, mixed, mix_gain, final_w, gate, "hij,hc->ijc")


def local(
    pair,
    residue_count,
    out_norm,
    out_proj,
    out_gate,
    out_mix_norm,
    out_final,
    inc_norm,
    inc_proj,
    inc_gate,
    inc_mix_norm,
    inc_final,
    transition_norm,
    transition_up,
    transition_down,
):
    tile_rows = pair.shape[0]
    tile_cols = pair.shape[1]
    row_place = lax.axis_index("row") * tile_rows + jnp.arange(tile_rows, dtype=jnp.int32)
    col_place = lax.axis_index("col") * tile_cols + jnp.arange(tile_cols, dtype=jnp.int32)
    valid_rows = (row_place < residue_count[0]).astype(jnp.float32)
    valid_cols = (col_place < residue_count[0]).astype(jnp.float32)
    mask = valid_rows[:, None] * valid_cols[None, :]
    after_one = triangle(pair, out_norm, out_proj, out_gate, out_mix_norm, out_final, mask, False)
    after_two = triangle(
        after_one, inc_norm, inc_proj, inc_gate, inc_mix_norm, inc_final, mask, True
    )
    normed = layer_norm(after_two.astype(jnp.float32), transition_norm, -1).astype(jnp.bfloat16)
    width = transition_down.shape[0]
    total = jnp.zeros(after_two.shape, jnp.float32)
    for offset in range(0, width, 128):
        gate_part = jnp.einsum(
            "ijc,cf->ijf",
            normed,
            transition_up[:, offset : offset + 128],
            preferred_element_type=jnp.float32,
        )
        value_part = jnp.einsum(
            "ijc,cf->ijf",
            normed,
            transition_up[:, width + offset : width + offset + 128],
            preferred_element_type=jnp.float32,
        )
        inner = (jax.nn.silu(gate_part) * value_part).astype(jnp.bfloat16)
        total = total + jnp.einsum(
            "ijf,fc->ijc",
            inner,
            transition_down[offset : offset + 128],
            preferred_element_type=jnp.float32,
        )
    return (after_two.astype(jnp.float32) + total).astype(jnp.bfloat16)


def solution(mesh):
    placed = (
        P(("parts", "row"), "col", None),
        P("parts"),
        P(),
        P(),
        P(),
        P(),
        P(),
        P(),
        P(),
        P(),
        P(),
        P(),
        P(),
        P(),
        P(),
    )
    return jax.shard_map(
        local,
        mesh=mesh,
        in_specs=placed,
        out_specs=P(("parts", "row"), "col", None),
        check_vma=False,
    )
```

profile of v0, /device:TPU:0, one launch (start us, length us, event | category | flops | bytes accessed | tf_op | source)
XLA Modules:
  0.0 116.0 jit_solution(1480908070667486916)
XLA Ops:
  0.0 1.1 convert_reduce_fusion
  1.1 1.2 %fusion.21 = f32[24,24]{1,0:T(8,128)S(1)} fusion(bf16[24,24,128]{2,1,0:T(8,128)(2,1)} %param.15, f32[24,24]{1,0:T(8,128)S(1)} %broadcast_multiply_fusion.5), kind=kLoop, calls=%fused_computation.46 | loop fusion | flops 294336 | bytes 152064 | tf_op jit(solution)/shard_map/reduce_sum | solution.py:10
  2.3 1.3 %convolution_bitcast_fusion.2 = f32[256,24,24]{0,2,1:T(8,128)S(1)} fusion(bf16[128,512]{1,0:T(8,128)(2,1)} %param.18, bf16[24,24,128]{2,1,0:T(8,128)(2,1)} %param.15, f32[128]{0:T(128)} %param.17, f32[24,24]{1,0:T(8,128)S(1)} %add_rsqrt_fusion.4, f32[24,24]{1,0:T(8,128)S(1)} %broadcast_multiply_fusion.5), kind=kOutput, calls=%fused_computation.4 | convolution fusion | flops 38117376 | bytes 807936 | tf_op jit(solution)/shard_map/ijc,cf->fij/dot_general | solution.py:21
  3.6 1.3 %convolution_bitcast_fusion.3 = f32[256,24,24]{0,2,1:T(8,128)S(1)} fusion(bf16[128,512]{1,0:T(8,128)(2,1)} %param.18, bf16[24,24,128]{2,1,0:T(8,128)(2,1)} %param.15, f32[128]{0:T(128)} %param.17, f32[24,24]{1,0:T(8,128)S(1)} %add_rsqrt_fusion.4, f32[24,24]{1,0:T(8,128)S(1)} %broadcast_multiply_fusion.5), kind=kOutput, calls=%fused_computation.5 | convolution fusion | flops 38117376 | bytes 807936 | tf_op jit(solution)/shard_map/ijc,cf->fij/dot_general | solution.py:17
  6.2 1.6 %reshape.144 = bf16[4,2,9216]{2,1,0:T(2,128)(2,1)} reshape(bf16[128,24,24]{2,1,0:T(8,128)(2,1)S(1)} %copy.69) | data formatting | bytes 294912
  7.9 6.3 %all-to-all-start.1 = ((bf16[4,2,9216]{2,1,0:T(2,128)(2,1)}), bf16[4,2,9216]{2,1,0:T(2,128)(2,1)S(1)}, u32[]{:S(2)}, u32[]{:S(2)}) async-start(bf16[4,2,9216]{2,1,0:T(2,128)(2,1)} %reshape.144), calls=%async_computation.1 | async-start | bytes 294912 | tf_op jit(solution)/shard_map/all_to_all | solution.py:40
  14.6 1.7 %reshape.142 = bf16[4,2,9216]{2,1,0:T(2,128)(2,1)} reshape(bf16[128,24,24]{2,1,0:T(8,128)(2,1)S(1)} %copy.67) | data formatting | bytes 294912
  16.3 4.2 %all-to-all-done.1 = bf16[4,2,9216]{2,1,0:T(2,128)(2,1)S(1)} async-done(((bf16[4,2,9216]{2,1,0:T(2,128)(2,1)}), bf16[4,2,9216]{2,1,0:T(2,128)(2,1)S(1)}, u32[]{:S(2)}, u32[]{:S(2)}) %all-to-all-start.1) | async-done | bytes 147488 | tf_op jit(solution)/shard_map/all_to_all | solution.py:40
  20.4 3.3 %all-to-all-start = ((bf16[4,2,9216]{2,1,0:T(2,128)(2,1)}), bf16[4,2,9216]{2,1,0:T(2,128)(2,1)S(1)}, u32[]{:S(2)}, u32[]{:S(2)}) async-start(bf16[4,2,9216]{2,1,0:T(2,128)(2,1)} %reshape.142), calls=%async_computation | async-start | bytes 294912 | tf_op jit(solution)/shard_map/all_to_all | solution.py:39
  23.8 1.1 reshape.145
  25.9 8.6 %all_gather.6 = bf16[32,96,96]{2,1,0:T(8,128)(2,1)S(1)} all-gather(bf16[32,24,96]{2,1,0:T(8,128)(2,1)S(1)} %all_to_all.86), channel_id=1, replica_groups=mesh['parts'=2,'row'=4,'col'=4] {'row'}, dimensions={1}, use_global_device_ids=true | all-gather | bytes 737280 | tf_op jit(solution)/shard_map/all_gather | solution.py:54
  34.5 1.1 reshape.143
  37.6 1.2 %reshape.146 = bf16[4,2,9216]{2,1,0:T(2,128)(2,1)} reshape(bf16[96,24,32]{2,1,0:T(8,128)(2,1)S(1)} %bitcast.142) | data formatting | bytes 294912
  38.8 5.1 %all-to-all-start.2 = ((bf16[4,2,9216]{2,1,0:T(2,128)(2,1)}), bf16[4,2,9216]{2,1,0:T(2,128)(2,1)S(1)}, u32[]{:S(2)}, u32[]{:S(2)}) async-start(bf16[4,2,9216]{2,1,0:T(2,128)(2,1)} %reshape.146), calls=%async_computation.2 | async-start | bytes 294912 | tf_op jit(solution)/shard_map/all_to_all | solution.py:57
  44.3 6.2 %all-to-all-done.2 = bf16[4,2,9216]{2,1,0:T(2,128)(2,1)S(1)} async-done(((bf16[4,2,9216]{2,1,0:T(2,128)(2,1)}), bf16[4,2,9216]{2,1,0:T(2,128)(2,1)S(1)}, u32[]{:S(2)}, u32[]{:S(2)}) %all-to-all-start.2) | async-done | bytes 147488 | tf_op jit(solution)/shard_map/all_to_all | solution.py:57
  54.8 1.1 fusion.129
  57.6 1.7 %reshape.148 = bf16[4,2,9216]{2,1,0:T(2,128)(2,1)} reshape(bf16[128,24,24]{2,1,0:T(8,128)(2,1)S(1)} %copy.74) | data formatting | bytes 294912
  59.2 3.3 %all-to-all-start.3 = ((bf16[4,2,9216]{2,1,0:T(2,128)(2,1)}), bf16[4,2,9216]{2,1,0:T(2,128)(2,1)S(1)}, u32[]{:S(2)}, u32[]{:S(2)}) async-start(bf16[4,2,9216]{2,1,0:T(2,128)(2,1)} %reshape.148), calls=%async_computation.3 | async-start | bytes 294912 | tf_op jit(solution)/shard_map/all_to_all | solution.py:39
  63.0 1.6 %reshape.152 = bf16[4,2,9216]{2,1,0:T(2,128)(2,1)} reshape(bf16[128,24,24]{2,1,0:T(8,128)(2,1)S(1)} %copy.79) | data formatting | bytes 294912
  64.6 3.9 %all-to-all-done.3 = bf16[4,2,9216]{2,1,0:T(2,128)(2,1)S(1)} async-done(((bf16[4,2,9216]{2,1,0:T(2,128)(2,1)}), bf16[4,2,9216]{2,1,0:T(2,128)(2,1)S(1)}, u32[]{:S(2)}, u32[]{:S(2)}) %all-to-all-start.3) | async-done | bytes 147488 | tf_op jit(solution)/shard_map/all_to_all | solution.py:39
  68.5 3.3 %all-to-all-start.5 = ((bf16[4,2,9216]{2,1,0:T(2,128)(2,1)}), bf16[4,2,9216]{2,1,0:T(2,128)(2,1)S(1)}, u32[]{:S(2)}, u32[]{:S(2)}) async-start(bf16[4,2,9216]{2,1,0:T(2,128)(2,1)} %reshape.152), calls=%async_computation.5 | async-start | bytes 294912 | tf_op jit(solution)/shard_map/all_to_all | solution.py:40
  71.8 1.1 reshape.149
  73.5 2.0 %copy.84 = bf16[32,24,4,24]{0,1,3,2:T(8,128)(2,1)S(1)} copy(bf16[32,24,4,24]{3,2,1,0:T(4,128)(2,1)S(1)} %bitcast.139) | data formatting | bytes 294912 | tf_op jit(solution)/shard_map/all_to_all | solution.py:39
  75.5 1.2 %reshape.150 = bf16[4,2,9216]{2,1,0:T(2,128)(2,1)} reshape(bf16[96,24,32]{2,1,0:T(8,128)(2,1)S(1)} %bitcast.146) | data formatting | bytes 294912
  77.8 3.6 %all-to-all-start.4 = ((bf16[4,2,9216]{2,1,0:T(2,128)(2,1)}), bf16[4,2,9216]{2,1,0:T(2,128)(2,1)S(1)}, u32[]{:S(2)}, u32[]{:S(2)}) async-start(bf16[4,2,9216]{2,1,0:T(2,128)(2,1)} %reshape.150), calls=%async_computation.4 | async-start | bytes 294912 | tf_op jit(solution)/shard_map/all_to_all | solution.py:43
  81.3 1.1 reshape.153
  83.4 8.9 %all_gather.7 = bf16[32,96,96]{2,1,0:T(8,128)(2,1)S(1)} all-gather(bf16[32,24,96]{2,1,0:T(8,128)(2,1)S(1)} %all_to_all.99), channel_id=1, replica_groups=mesh['parts'=2,'row'=4,'col'=4] {'row'}, dimensions={1}, use_global_device_ids=true | all-gather | bytes 737280 | tf_op jit(solution)/shard_map/all_gather | solution.py:47
  94.5 1.2 %reshape.154 = bf16[4,2,9216]{2,1,0:T(2,128)(2,1)} reshape(bf16[96,24,32]{2,1,0:T(8,128)(2,1)S(1)} %bitcast.144) | data formatting | bytes 294912
  95.8 4.1 %all-to-all-start.6 = ((bf16[4,2,9216]{2,1,0:T(2,128)(2,1)}), bf16[4,2,9216]{2,1,0:T(2,128)(2,1)S(1)}, u32[]{:S(2)}, u32[]{:S(2)}) async-start(bf16[4,2,9216]{2,1,0:T(2,128)(2,1)} %reshape.154), calls=%async_computation.6 | async-start | bytes 294912 | tf_op jit(solution)/shard_map/all_to_all | solution.py:57
  100.1 6.4 %all-to-all-done.6 = bf16[4,2,9216]{2,1,0:T(2,128)(2,1)S(1)} async-done(((bf16[4,2,9216]{2,1,0:T(2,128)(2,1)}), bf16[4,2,9216]{2,1,0:T(2,128)(2,1)S(1)}, u32[]{:S(2)}, u32[]{:S(2)}) %all-to-all-start.6) | async-done | bytes 147488 | tf_op jit(solution)/shard_map/all_to_all | solution.py:57
  112.2 1.0 fusion.95
  114.9 1.1 fusion.17
  (90 shorter events, 22.8 us)
Async XLA Ops:
  0.0 54.8 %copy-start = (bf16[128,128]{1,0:T(8,128)(2,1)S(1)}, bf16[128,128]{1,0:T(8,128)(2,1)}, u32[]{:S(2)}) copy-start(bf16[128,128]{1,0:T(8,128)(2,1)} %param.21) | copy-start | bytes 98308
  7.9 12.6 %all-to-all-start.1 = ((bf16[4,2,9216]{2,1,0:T(2,128)(2,1)}), bf16[4,2,9216]{2,1,0:T(2,128)(2,1)S(1)}, u32[]{:S(2)}, u32[]{:S(2)}) async-start(bf16[4,2,9216]{2,1,0:T(2,128)(2,1)} %reshape.144), calls=%async_computation.1 | async-start | bytes 294912 | tf_op jit(solution)/shard_map/all_to_all | solution.py:40
  20.4 14.1 %all-to-all-start = ((bf16[4,2,9216]{2,1,0:T(2,128)(2,1)}), bf16[4,2,9216]{2,1,0:T(2,128)(2,1)S(1)}, u32[]{:S(2)}, u32[]{:S(2)}) async-start(bf16[4,2,9216]{2,1,0:T(2,128)(2,1)} %reshape.142), calls=%async_computation | async-start | bytes 294912 | tf_op jit(solution)/shard_map/all_to_all | solution.py:39
  36.6 7.2 %copy-start.1 = (bf16[24,24,128]{2,1,0:T(8,128)(2,1)S(1)}, bf16[24,24,128]{2,1,0:T(8,128)(2,1)}, u32[]{:S(2)}) copy-start(bf16[24,24,128]{2,1,0:T(8,128)(2,1)} %param.15) | copy-start | bytes 442372
  36.7 7.2 %copy-start.5 = (f32[128]{0:T(128)S(1)}, f32[128]{0:T(128)}, u32[]{:S(2)}) copy-start(f32[128]{0:T(128)} %param.17) | copy-start | bytes 1540
  36.7 7.2 %copy-start.11 = (bf16[128,128]{1,0:T(8,128)(2,1)S(1)}, bf16[128,128]{1,0:T(8,128)(2,1)}, u32[]{:S(2)}) copy-start(bf16[128,128]{1,0:T(8,128)(2,1)} %param.19) | copy-start | bytes 98308
  38.8 11.7 %all-to-all-start.2 = ((bf16[4,2,9216]{2,1,0:T(2,128)(2,1)}), bf16[4,2,9216]{2,1,0:T(2,128)(2,1)S(1)}, u32[]{:S(2)}, u32[]{:S(2)}) async-start(bf16[4,2,9216]{2,1,0:T(2,128)(2,1)} %reshape.146), calls=%async_computation.2 | async-start | bytes 294912 | tf_op jit(solution)/shard_map/all_to_all | solution.py:57
  53.4 1.4 %copy-start.6 = (f32[128]{0:T(128)S(1)}, f32[128]{0:T(128)}, u32[]{:S(2)}) copy-start(f32[128]{0:T(128)} %param.20) | copy-start | bytes 1540
  54.2 2.0 %copy-start.8 = (f32[128]{0:T(128)S(1)}, f32[128]{0:T(128)}, u32[]{:S(2)}) copy-start(f32[128]{0:T(128)} %param.22) | copy-start | bytes 1540
  54.2 2.2 %copy-start.2 = (bf16[128,512]{1,0:T(8,128)(2,1)S(1)}, bf16[128,512]{1,0:T(8,128)(2,1)}, u32[]{:S(2)}) copy-start(bf16[128,512]{1,0:T(8,128)(2,1)} %param.23) | copy-start | bytes 393220
  59.2 9.3 %all-to-all-start.3 = ((bf16[4,2,9216]{2,1,0:T(2,128)(2,1)}), bf16[4,2,9216]{2,1,0:T(2,128)(2,1)S(1)}, u32[]{:S(2)}, u32[]{:S(2)}) async-start(bf16[4,2,9216]{2,1,0:T(2,128)(2,1)} %reshape.148), calls=%async_computation.3 | async-start | bytes 294912 | tf_op jit(solution)/shard_map/all_to_all | solution.py:39
  68.5 9.3 %all-to-all-start.5 = ((bf16[4,2,9216]{2,1,0:T(2,128)(2,1)}), bf16[4,2,9216]{2,1,0:T(2,128)(2,1)S(1)}, u32[]{:S(2)}, u32[]{:S(2)}) async-start(bf16[4,2,9216]{2,1,0:T(2,128)(2,1)} %reshape.152), calls=%async_computation.5 | async-start | bytes 294912 | tf_op jit(solution)/shard_map/all_to_all | solution.py:40
  77.8 14.6 %all-to-all-start.4 = ((bf16[4,2,9216]{2,1,0:T(2,128)(2,1)}), bf16[4,2,9216]{2,1,0:T(2,128)(2,1)S(1)}, u32[]{:S(2)}, u32[]{:S(2)}) async-start(bf16[4,2,9216]{2,1,0:T(2,128)(2,1)} %reshape.150), calls=%async_computation.4 | async-start | bytes 294912 | tf_op jit(solution)/shard_map/all_to_all | solution.py:43
  93.8 6.0 %copy-start.12 = (bf16[128,128]{1,0:T(8,128)(2,1)S(1)}, bf16[128,128]{1,0:T(8,128)(2,1)}, u32[]{:S(2)}) copy-start(bf16[128,128]{1,0:T(8,128)(2,1)} %param.24) | copy-start | bytes 98308
  95.8 10.7 %all-to-all-start.6 = ((bf16[4,2,9216]{2,1,0:T(2,128)(2,1)}), bf16[4,2,9216]{2,1,0:T(2,128)(2,1)S(1)}, u32[]{:S(2)}, u32[]{:S(2)}) async-start(bf16[4,2,9216]{2,1,0:T(2,128)(2,1)} %reshape.154), calls=%async_computation.6 | async-start | bytes 294912 | tf_op jit(solution)/shard_map/all_to_all | solution.py:57
  108.7 1.4 %copy-start.4 = (bf16[128,128]{1,0:T(8,128)(2,1)S(1)}, bf16[128,128]{1,0:T(8,128)(2,1)}, u32[]{:S(2)}) copy-start(bf16[128,128]{1,0:T(8,128)(2,1)} %param.26) | copy-start | bytes 98308
  108.8 1.4 %copy-start.7 = (f32[128]{0:T(128)S(1)}, f32[128]{0:T(128)}, u32[]{:S(2)}) copy-start(f32[128]{0:T(128)} %param.25) | copy-start | bytes 1540
  109.6 1.3 %copy-start.9 = (f32[128]{0:T(128)S(1)}, f32[128]{0:T(128)}, u32[]{:S(2)}) copy-start(f32[128]{0:T(128)} %param.27) | copy-start | bytes 1540
  110.2 3.0 %copy-start.3 = (bf16[128,1024]{1,0:T(8,128)(2,1)S(1)}, bf16[128,1024]{1,0:T(8,128)(2,1)}, u32[]{:S(2)}) copy-start(bf16[128,1024]{1,0:T(8,128)(2,1)} %param.28) | copy-start | bytes 786436
  110.6 3.0 %copy-start.10 = (bf16[512,128]{1,0:T(8,128)(2,1)S(1)}, bf16[512,128]{1,0:T(8,128)(2,1)}, u32[]{:S(2)}) copy-start(bf16[512,128]{1,0:T(8,128)(2,1)} %param.29) | copy-start | bytes 393220
where the time goes:
time: 117 us; the launch traced here: 116 us
  local copies, waits for them, and re-layouts  29.6 us (25%)
  starting transfers between devices  29 us (25%)
  waiting for transfers between devices  21.7 us (19%)
  blocking collectives  17.5 us (15%)
  matrix products  10.8 us (9%)
  other arithmetic  6.03 us (5%)
  between operations  1.35 us (1%)
    all_gather x2, blocking collectives, mix_over_col(): lax.all_gather(right_wide, 'row', axis=1, tiled=True)  17.5 us
    unnamed x40, local copies, waits for them, and re-layouts  15.5 us
    all_to_all x2, waiting for transfers between devices, mix_over_col(): lax.all_to_all(mixed.astype(jnp.bfloat16), 'col', split_axis=2, concat_ax...  12.6 us
    all_to_all x2, starting transfers between devices, mix_over_col(): lax.all_to_all(right, 'col', split_axis=0, concat_axis=2, tiled=True)  9.65 us
    all_to_all x2, starting transfers between devices, mix_over_col(): lax.all_to_all(mixed.astype(jnp.bfloat16), 'col', split_axis=2, concat_ax...  9.14 us
    all_to_all x2, starting transfers between devices, mix_over_col(): lax.all_to_all(left, 'col', split_axis=0, concat_axis=2, tiled=True)  6.67 us
    all_to_all x2, waiting for transfers between devices, mix_over_col(): lax.all_to_all(right, 'col', split_axis=0, concat_axis=2, tiled=True)  5.15 us
    convert_element_type x6, local copies, waits for them, and re-layouts, finish(): mixed.astype(jnp.float32)  4.06 us
  transfers between devices with their start and end apart: 7, of which 5 were waited for; matrix products, arithmetic and copies ran while one was open for 11% of the time, Pallas kernels for 0%

commit v1 on v0

--- a/solution.py
+++ b/solution.py
@@ -1,7 +1,13 @@
+import functools
+
 import jax
 import jax.numpy as jnp
 from jax import lax
+from jax.experimental import pallas as pl
+from jax.experimental.pallas import tpu as pltpu
 from jax.sharding import PartitionSpec as P
+
+MESH = pl.DeviceIdType.MESH
 
 
 def layer_norm(values, gain, axis):
@@ -65,7 +71,7 @@
     return finish(current, mixed, mix_gain, final_w, gate, "hij,hc->ijc")
 
 
-def local(
+def local_plain(
     pair,
     residue_count,
     out_norm,
@@ -119,6 +125,296 @@
     return (after_two.astype(jnp.float32) + total).astype(jnp.bfloat16)
 
 
+def norm_rows(values, gain):
+    mean = jnp.mean(values, axis=-1, keepdims=True)
+    centred = values - mean
+    spread = jnp.mean(centred * centred, axis=-1, keepdims=True)
+    return centred * lax.rsqrt(spread + 1e-05) * gain
+
+
+def matmul(left, right):
+    return jnp.dot(left, right, preferred_element_type=jnp.float32)
+
+
+def masked_half(normed, proj_ref, start, hidden, mask):
+    part = matmul(normed, proj_ref[:, start : start + 2 * hidden])
+    return (mask * jax.nn.sigmoid(part[:, :hidden]) * part[:, hidden:]).astype(jnp.bfloat16)
+
+
+def contract(size, left_ref, right_ref, out_ref, out_slot):
+    for first in range(0, size, 8):
+
+        def step(k, totals, first=first):
+            base = pl.multiple_of(k * size, 8)
+            block = right_ref[pl.ds(base, size), :]
+            return tuple(
+                total + left_ref[pl.ds(base + first + place, 1), :] * block
+                for place, total in enumerate(totals)
+            )
+
+        zero = jnp.zeros((size, right_ref.shape[1]), jnp.float32)
+        totals = lax.fori_loop(0, size, step, (zero,) * 8, unroll=2)
+        out_ref[out_slot, first * size : (first + 8) * size, :] = jnp.concatenate(
+            totals, axis=0
+        ).astype(jnp.bfloat16)
+
+
+def block_kernel(
+    size,
+    n_row,
+    n_col,
+    count_ref,
+    pair_ref,
+    out_norm,
+    out_proj,
+    out_gate,
+    out_mix_norm,
+    out_final,
+    inc_norm,
+    inc_proj,
+    inc_gate,
+    inc_mix_norm,
+    inc_final,
+    transition_norm,
+    transition_up,
+    transition_down,
+    result_ref,
+    turn_a,
+    turn_b,
+    wide_left,
+    wide_right,
+    right_in,
+    part_out,
+    part_in,
+    left_in,
+    sum_out,
+    sum_in,
+    send_a,
+    recv_a,
+    send_b,
+    recv_b,
+    send_c,
+    recv_c,
+    send_d,
+    recv_d,
+):
+    row = lax.axis_index("row")
+    col = lax.axis_index("col")
+    tokens = size * size
+    hidden = out_proj.shape[1] // 4
+
+    def row_peer(step):
+        place = (row // 2 + step // 2) % (n_row // 2)
+        return place * 2 + (row % 2 + step % 2) % 2
+
+    def col_peer(step):
+        return (col + step) % n_col
+
+    barrier = pltpu.get_barrier_semaphore()
+    for step in range(1, n_row):
+        pl.semaphore_signal(
+            barrier, inc=1, device_id={"row": row_peer(step)}, device_id_type=MESH
+        )
+    for step in range(1, n_col):
+        pl.semaphore_signal(
+            barrier, inc=1, device_id={"col": col_peer(step)}, device_id_type=MESH
+        )
+
+    def copy(source, target, send, recv, where):
+        return pltpu.make_async_remote_copy(
+            src_ref=source,
+            dst_ref=target,
+            send_sem=send,
+            recv_sem=recv,
+            device_id=where,
+            device_id_type=MESH,
+        )
+
+    def to_row(step):
+        return copy(
+            right_in.at[0], right_in.at[step], send_a.at[step], recv_a.at[step],
+            {"row": row_peer(step)},
+        )
+
+    def to_owner(step):
+        return copy(
+            part_out.at[step], part_in.at[col], send_b.at[step], recv_b.at[col],
+            {"col": row_peer(step)},
+        )
+
+    def from_col(sender):
+        return copy(
+            part_out.at[0], part_in.at[sender], send_b.at[0], recv_b.at[sender],
+            {"col": sender},
+        )
+
+    def to_col(step):
+        return copy(
+            left_in.at[col], left_in.at[col], send_c.at[step], recv_c.at[col],
+            {"col": col_peer(step)},
+        )
+
+    def left_from(sender):
+        return copy(
+            left_in.at[col], left_in.at[sender], send_c.at[0], recv_c.at[sender],
+            {"col": sender},
+        )
+
+    def to_row_owner(step):
+        return copy(
+            sum_out.at[step], sum_in.at[row], send_d.at[step], recv_d.at[row],
+            {"row": col_peer(step)},
+        )
+
+    def from_row(sender):
+        return copy(
+            sum_out.at[0], sum_in.at[sender], send_d.at[0], recv_d.at[sender],
+            {"row": sender},
+        )
+
+    shape = (size, size, hidden)
+    first = lax.broadcasted_iota(jnp.int32, shape, 0)
+    second = lax.broadcasted_iota(jnp.int32, shape, 1)
+    count = count_ref[0]
+
+    def mask_of(a, b):
+        real = jnp.logical_and(a < count, b < count)
+        return jnp.where(real, 1.0, 0.0).astype(jnp.float32).reshape(tokens, hidden)
+
+    mask = mask_of(first + row * size, second + col * size)
+    mask_turned = mask_of(first + col * size, second + row * size)
+
+    normed = norm_rows(pair_ref[...].astype(jnp.float32), out_norm[...])
+    turn_a[...] = normed
+    for k in range(size):
+        turn_b[k * size : (k + 1) * size, :] = turn_a[pl.ds(k, size, stride=size), :]
+    turned = turn_b[...].astype(jnp.bfloat16)
+    right_in[0] = masked_half(turned, out_proj, 2 * hidden, hidden, mask_turned)
+    pl.semaphore_wait(barrier, n_row + n_col - 2)
+    for step in range(1, n_row):
+        to_row(step).start()
+    wide_left[...] = masked_half(turned, out_proj, 0, hidden, mask_turned).astype(jnp.float32)
+    for step in range(n_row):
+        if step > 0:
+            to_row(step).wait_recv()
+        wide_right[...] = right_in[step].astype(jnp.float32)
+        contract(size, wide_left, wide_right, part_out, step)
+
+        @pl.when(row_peer(step) != col)
+        def _():
+            to_owner(step).start()
+
+        @pl.when(row_peer(step) == col)
+        def _():
+            part_in[col] = part_out[step]
+
+    gate = jax.nn.sigmoid(matmul(normed.astype(jnp.bfloat16), out_gate[...]))
+    for sender in range(n_col):
+
+        @pl.when(sender != col)
+        def _():
+            from_col(sender).wait_recv()
+
+    mixed = part_in[0].astype(jnp.float32)
+    for sender in range(1, n_col):
+        mixed = mixed + part_in[sender].astype(jnp.float32)
+    mixed = norm_rows(mixed.astype(jnp.bfloat16).astype(jnp.float32), out_mix_norm[...])
+    change = matmul(mixed.astype(jnp.bfloat16), out_final[...])
+    after = (pair_ref[...].astype(jnp.float32) + gate * change).astype(jnp.bfloat16)
+    after = after.astype(jnp.float32)
+
+    normed = norm_rows(after, inc_norm[...]).astype(jnp.bfloat16)
+    left_in[col] = masked_half(normed, inc_proj, 0, hidden, mask)
+    for step in range(1, n_col):
+        to_col(step).start()
+    wide_right[...] = masked_half(normed, inc_proj, 2 * hidden, hidden, mask).astype(jnp.float32)
+    gate = jax.nn.sigmoid(matmul(normed, inc_gate[...]))
+    turn_a[...] = after
+    turn_b[...] = gate
+    for step in (0, 1, 3, 2):
+        owner = col_peer(step)
+        if step > 0:
+            left_from(owner).wait_recv()
+        wide_left[...] = left_in[owner].astype(jnp.float32)
+        contract(size, wide_left, wide_right, sum_out, step)
+
+        @pl.when(owner != row)
+        def _():
+            to_row_owner(step).start()
+
+        @pl.when(owner == row)
+        def _():
+            sum_in[row] = sum_out[step]
+
+    for sender in range(n_row):
+
+        @pl.when(sender != row)
+        def _():
+            from_row(sender).wait_recv()
+
+    mixed = sum_in[0].astype(jnp.float32)
+    for sender in range(1, n_row):
+        mixed = mixed + sum_in[sender].astype(jnp.float32)
+    mixed = norm_rows(mixed.astype(jnp.bfloat16).astype(jnp.float32), inc_mix_norm[...])
+    change = matmul(mixed.astype(jnp.bfloat16), inc_final[...])
+    after = (turn_a[...] + turn_b[...] * change).astype(jnp.bfloat16).astype(jnp.float32)
+
+    normed = norm_rows(after, transition_norm[...]).astype(jnp.bfloat16)
+    width = transition_down.shape[0]
+    total = jnp.zeros((tokens, hidden), jnp.float32)
+    for offset in range(0, width, 256):
+        lifted = matmul(normed, transition_up[:, offset : offset + 256])
+        value = matmul(normed, transition_up[:, width + offset : width + offset + 256])
+        inner = (lifted * jax.nn.sigmoid(lifted) * value).astype(jnp.bfloat16)
+        total = total + matmul(inner, transition_down[offset : offset + 256, :])
+    result_ref[...] = (after + total.astype(jnp.bfloat16).astype(jnp.float32)).astype(jnp.bfloat16)
+
+    for step in range(1, n_row):
+        to_row(step).wait_send()
+    for step in range(n_row):
+
+        @pl.when(row_peer(step) != col)
+        def _():
+            to_owner(step).wait_send()
+
+    for step in range(1, n_col):
+        to_col(step).wait_send()
+    for step in range(n_col):
+
+        @pl.when(col_peer(step) != row)
+        def _():
+            to_row_owner(step).wait_send()
+
+
+def local_kernel(n_row, n_col, pair, residue_count, *rest):
+    size, _, channels = pair.shape
+    tokens = size * size
+    rest = [leaf[None, :] if leaf.ndim == 1 else leaf for leaf in rest]
+    vmem = pl.BlockSpec(memory_space=pltpu.VMEM)
+    narrow = pltpu.VMEM((4, tokens, channels), jnp.bfloat16)
+    wide = pltpu.VMEM((tokens, channels), jnp.float32)
+    result = pl.pallas_call(
+        functools.partial(block_kernel, size, n_row, n_col),
+        out_shape=jax.ShapeDtypeStruct((tokens, channels), jnp.bfloat16),
+        in_specs=[pl.BlockSpec(memory_space=pltpu.SMEM)] + [vmem] * (1 + len(rest)),
+        out_specs=vmem,
+        scratch_shapes=[wide] * 4 + [narrow] * 6 + [pltpu.SemaphoreType.DMA((4,))] * 8,
+        compiler_params=pltpu.CompilerParams(
+            collective_id=0, has_side_effects=True, vmem_limit_bytes=48 * 1024 * 1024
+        ),
+    )(residue_count, pair.reshape(tokens, channels), *rest)
+    return result.reshape(size, size, channels)
+
+
+def local(pair, residue_count, *rest, n_row, n_col):
+    hidden = rest[1].shape[1] // 4
+    fits = n_row == 4 and n_col == 4 and pair.shape[0] == pair.shape[1]
+    fits = fits and pair.shape[0] % 8 == 0 and pair.shape[0] <= 32
+    if fits and hidden == pair.shape[2] and hidden % 128 == 0:
+        return local_kernel(n_row, n_col, pair, residue_count, *rest)
+    return local_plain(pair, residue_count, *rest)
+
+
 def solution(mesh):
     placed = (
         P(("parts", "row"), "col", None),
@@ -138,7 +434,9 @@
         P(),
     )
     return jax.shard_map(
-        local,
+        functools.partial(
+            local, n_row=mesh.shape["row"], n_col=mesh.shape["col"]
+        ),
         mesh=mesh,
         in_specs=placed,
         out_specs=P(("parts", "row"), "col", None),

time: 117 us -> 60.3 us (0.52)
  the two profiles are of different devices: /device:TPU:0 before, /device:TPU:27 now
where the time goes in v1:
time: 60.3 us; the launch traced here: 59.8 us
  Pallas kernels  50.1 us (83%)
  local copies, waits for them, and re-layouts  8.94 us (15%)
  between operations  0.71 us (1%)
    pallas_call x1, Pallas kernels, local_kernel(): pl.pallas_call(functools.partial(block_kernel, size, n_row, n_col), out_s...  50.1 us
    unnamed x29, local copies, waits for them, and re-layouts  8.94 us

profile of v1, /device:TPU:27, one launch (start us, length us, event | category | flops | bytes accessed | tf_op | source)
XLA Modules:
  0.0 59.8 jit_solution(18257771556265992211)
XLA Ops:
  0.7 0.0 copy-start.12
  0.7 0.0 copy-start.13
  0.7 0.0 copy-start.9
  0.7 0.0 copy-start.10
  0.7 0.0 copy-start.11
  0.7 0.6 %copy-done.12 = f32[128]{0:T(128)S(1)} copy-done((f32[128]{0:T(128)S(1)}, f32[128]{0:T(128)}, u32[]{:S(2)}) %copy-start.12) | copy-done | bytes 536
  1.3 0.0 copy-done.13
  1.3 0.0 copy-done.9
  1.3 0.0 copy-done.10
  1.4 0.0 copy-done.11
  1.4 0.0 copy-start
  1.4 0.9 %copy-done = bf16[128,1024]{1,0:T(8,128)(2,1)S(1)} copy-done((bf16[128,1024]{1,0:T(8,128)(2,1)S(1)}, bf16[128,1024]{1,0:T(8,128)(2,1)}, u32[]{:S(2)}) %copy-start) | copy-done | bytes 262168
  2.3 0.0 copy-start.1
  2.3 0.9 %copy-done.1 = bf16[24,24,128]{2,1,0:T(8,128)(2,1)S(1)} copy-done((bf16[24,24,128]{2,1,0:T(8,128)(2,1)S(1)}, bf16[24,24,128]{2,1,0:T(8,128)(2,1)}, u32[]{:S(2)}) %copy-start.1) | copy-done | bytes 147480
  3.2 0.0 copy-start.2
  3.2 0.9 %copy-done.2 = bf16[128,512]{1,0:T(8,128)(2,1)S(1)} copy-done((bf16[128,512]{1,0:T(8,128)(2,1)S(1)}, bf16[128,512]{1,0:T(8,128)(2,1)}, u32[]{:S(2)}) %copy-start.2) | copy-done | bytes 131096
  4.1 0.0 copy-start.3
  4.1 0.9 %copy-done.3 = bf16[128,512]{1,0:T(8,128)(2,1)S(1)} copy-done((bf16[128,512]{1,0:T(8,128)(2,1)S(1)}, bf16[128,512]{1,0:T(8,128)(2,1)}, u32[]{:S(2)}) %copy-start.3) | copy-done | bytes 131096
  5.0 0.0 copy-start.4
  5.0 0.9 %copy-done.4 = bf16[512,128]{1,0:T(8,128)(2,1)S(1)} copy-done((bf16[512,128]{1,0:T(8,128)(2,1)S(1)}, bf16[512,128]{1,0:T(8,128)(2,1)}, u32[]{:S(2)}) %copy-start.4) | copy-done | bytes 131096
  5.9 0.0 copy-start.5
  5.9 0.8 %copy-done.5 = bf16[128,128]{1,0:T(8,128)(2,1)S(1)} copy-done((bf16[128,128]{1,0:T(8,128)(2,1)S(1)}, bf16[128,128]{1,0:T(8,128)(2,1)}, u32[]{:S(2)}) %copy-start.5) | copy-done | bytes 32792
  6.7 0.0 copy-start.6
  6.7 0.8 %copy-done.6 = bf16[128,128]{1,0:T(8,128)(2,1)S(1)} copy-done((bf16[128,128]{1,0:T(8,128)(2,1)S(1)}, bf16[128,128]{1,0:T(8,128)(2,1)}, u32[]{:S(2)}) %copy-start.6) | copy-done | bytes 32792
  7.5 0.0 copy-start.7
  7.5 0.8 %copy-done.7 = bf16[128,128]{1,0:T(8,128)(2,1)S(1)} copy-done((bf16[128,128]{1,0:T(8,128)(2,1)S(1)}, bf16[128,128]{1,0:T(8,128)(2,1)}, u32[]{:S(2)}) %copy-start.7) | copy-done | bytes 32792
  8.2 0.0 copy-start.8
  8.2 0.8 %copy-done.8 = bf16[128,128]{1,0:T(8,128)(2,1)S(1)} copy-done((bf16[128,128]{1,0:T(8,128)(2,1)S(1)}, bf16[128,128]{1,0:T(8,128)(2,1)}, u32[]{:S(2)}) %copy-start.8) | copy-done | bytes 32792
  9.0 50.1 %shard_map.145 = bf16[576,128]{1,0:T(8,128)(2,1)S(1)} custom-call(s32[1]{0:T(128)S(6)} %copy.17.count_ref, bf16[576,128]{1,0:T(8,128)(2,1)S(1)} %bitcast.8, f32[1,128]{1,0:T(1,128)S(1)} %bitcast.9, bf16[128,512]{1,0:T(8,128)(2,1)S(1)} %copy-done.2, bf16[128,128]{1,0:T(8,128)(2,1)S(1)} %copy-done.5, f32[1,128]{1,0:T(1,128)S(1)} %bitcast.10, ...), custom_call_target="tpu_custom_call" | custom-call | tf_op jit(solution)/shard_map/pallas_call | solution.py:396
  59.1 0.7 %copy.18 = bf16[24,24,128]{2,1,0:T(8,128)(2,1)} copy(bf16[24,24,128]{2,1,0:T(8,128)(2,1)S(1)} %bitcast.7) | data formatting | bytes 294912
Async XLA Ops:
  0.7 0.7 %copy-start.12 = (f32[128]{0:T(128)S(1)}, f32[128]{0:T(128)}, u32[]{:S(2)}) copy-start(f32[128]{0:T(128)} %param.25) | copy-start | bytes 1540
  0.7 0.7 %copy-start.13 = (f32[128]{0:T(128)S(1)}, f32[128]{0:T(128)}, u32[]{:S(2)}) copy-start(f32[128]{0:T(128)} %param.27) | copy-start | bytes 1540
  0.7 0.7 %copy-start.9 = (f32[128]{0:T(128)S(1)}, f32[128]{0:T(128)}, u32[]{:S(2)}) copy-start(f32[128]{0:T(128)} %param.17) | copy-start | bytes 1540
  0.7 0.7 %copy-start.10 = (f32[128]{0:T(128)S(1)}, f32[128]{0:T(128)}, u32[]{:S(2)}) copy-start(f32[128]{0:T(128)} %param.20) | copy-start | bytes 1540
  0.7 0.7 %copy-start.11 = (f32[128]{0:T(128)S(1)}, f32[128]{0:T(128)}, u32[]{:S(2)}) copy-start(f32[128]{0:T(128)} %param.22) | copy-start | bytes 1540
  1.4 0.9 %copy-start = (bf16[128,1024]{1,0:T(8,128)(2,1)S(1)}, bf16[128,1024]{1,0:T(8,128)(2,1)}, u32[]{:S(2)}) copy-start(bf16[128,1024]{1,0:T(8,128)(2,1)} %transition_up.1) | copy-start | bytes 786436
  2.3 0.9 %copy-start.1 = (bf16[24,24,128]{2,1,0:T(8,128)(2,1)S(1)}, bf16[24,24,128]{2,1,0:T(8,128)(2,1)}, u32[]{:S(2)}) copy-start(bf16[24,24,128]{2,1,0:T(8,128)(2,1)} %param.15) | copy-start | bytes 442372
  3.2 0.9 %copy-start.2 = (bf16[128,512]{1,0:T(8,128)(2,1)S(1)}, bf16[128,512]{1,0:T(8,128)(2,1)}, u32[]{:S(2)}) copy-start(bf16[128,512]{1,0:T(8,128)(2,1)} %out_proj.1) | copy-start | bytes 393220
  4.1 0.9 %copy-start.3 = (bf16[128,512]{1,0:T(8,128)(2,1)S(1)}, bf16[128,512]{1,0:T(8,128)(2,1)}, u32[]{:S(2)}) copy-start(bf16[128,512]{1,0:T(8,128)(2,1)} %inc_proj.1) | copy-start | bytes 393220
  5.0 0.9 %copy-start.4 = (bf16[512,128]{1,0:T(8,128)(2,1)S(1)}, bf16[512,128]{1,0:T(8,128)(2,1)}, u32[]{:S(2)}) copy-start(bf16[512,128]{1,0:T(8,128)(2,1)} %transition_down.1) | copy-start | bytes 393220
  5.9 0.8 %copy-start.5 = (bf16[128,128]{1,0:T(8,128)(2,1)S(1)}, bf16[128,128]{1,0:T(8,128)(2,1)}, u32[]{:S(2)}) copy-start(bf16[128,128]{1,0:T(8,128)(2,1)} %out_gate.1) | copy-start | bytes 98308
  6.7 0.8 %copy-start.6 = (bf16[128,128]{1,0:T(8,128)(2,1)S(1)}, bf16[128,128]{1,0:T(8,128)(2,1)}, u32[]{:S(2)}) copy-start(bf16[128,128]{1,0:T(8,128)(2,1)} %out_final.1) | copy-start | bytes 98308
  7.5 0.8 %copy-start.7 = (bf16[128,128]{1,0:T(8,128)(2,1)S(1)}, bf16[128,128]{1,0:T(8,128)(2,1)}, u32[]{:S(2)}) copy-start(bf16[128,128]{1,0:T(8,128)(2,1)} %inc_gate.1) | copy-start | bytes 98308
  8.2 0.8 %copy-start.8 = (bf16[128,128]{1,0:T(8,128)(2,1)S(1)}, bf16[128,128]{1,0:T(8,128)(2,1)}, u32[]{:S(2)}) copy-start(bf16[128,128]{1,0:T(8,128)(2,1)} %inc_final.1) | copy-start | bytes 98308

commit v2 on v1

--- a/solution.py
+++ b/solution.py
@@ -164,44 +164,57 @@
     n_row,
     n_col,
     count_ref,
-    pair_ref,
-    out_norm,
-    out_proj,
-    out_gate,
-    out_mix_norm,
-    out_final,
-    inc_norm,
-    inc_proj,
-    inc_gate,
-    inc_mix_norm,
-    inc_final,
-    transition_norm,
-    transition_up,
-    transition_down,
-    result_ref,
-    turn_a,
-    turn_b,
-    wide_left,
-    wide_right,
-    right_in,
-    part_out,
-    part_in,
-    left_in,
-    sum_out,
-    sum_in,
-    send_a,
-    recv_a,
-    send_b,
-    recv_b,
-    send_c,
-    recv_c,
-    send_d,
-    recv_d,
+    *refs,
 ):
+    sources, result_ref, held, refs = refs[:14], refs[14], refs[15:29], refs[29:]
+    (
+        pair_ref,
+        out_norm,
+        out_proj,
+        out_gate,
+        out_mix_norm,
+        out_final,
+        inc_norm,
+        inc_proj,
+        inc_gate,
+        inc_mix_norm,
+        inc_final,
+        transition_norm,
+        transition_up,
+        transition_down,
+    ) = held
+    (
+        turn_a,
+        turn_b,
+        wide_left,
+        wide_right,
+        right_in,
+        part_out,
+        part_in,
+        left_in,
+        sum_out,
+        sum_in,
+        send_a,
+        recv_a,
+        send_b,
+        recv_b,
+        send_c,
+        recv_c,
+        send_d,
+        recv_d,
+        load,
+    ) = refs
     row = lax.axis_index("row")
     col = lax.axis_index("col")
     tokens = size * size
     hidden = out_proj.shape[1] // 4
+
+    loads = [
+        pltpu.make_async_copy(source, target, load.at[place])
+        for place, (source, target) in enumerate(zip(sources, held))
+    ]
+    for one in loads:
+        one.start()
 
     def row_peer(step):
         place = (row // 2 + step // 2) % (n_row // 2)
@@ -231,9 +244,10 @@
         )
 
     def to_row(step):
-        return copy(
-            right_in.at[0], right_in.at[step], send_a.at[step], recv_a.at[step],
-            {"row": row_peer(step)},
+        hop = 1 if step == 3 else step
+        return copy(
+            right_in.at[step - hop], right_in.at[step], send_a.at[step], recv_a.at[step],
+            {"row": row_peer(hop)},
         )
 
     def to_owner(step):
@@ -284,6 +298,8 @@
     mask = mask_of(first + row * size, second + col * size)
     mask_turned = mask_of(first + col * size, second + row * size)
 
+    for one in loads[:3]:
+        one.wait()
     normed = norm_rows(pair_ref[...].astype(jnp.float32), out_norm[...])
     turn_a[...] = normed
     for k in range(size):
@@ -291,12 +307,14 @@
     turned = turn_b[...].astype(jnp.bfloat16)
     right_in[0] = masked_half(turned, out_proj, 2 * hidden, hidden, mask_turned)
     pl.semaphore_wait(barrier, n_row + n_col - 2)
-    for step in range(1, n_row):
+    for step in (2, 1):
         to_row(step).start()
     wide_left[...] = masked_half(turned, out_proj, 0, hidden, mask_turned).astype(jnp.float32)
     for step in range(n_row):
         if step > 0:
             to_row(step).wait_recv()
+        if step == 2:
+            to_row(3).start()
         wide_right[...] = right_in[step].astype(jnp.float32)
         contract(size, wide_left, wide_right, part_out, step)
 
@@ -308,6 +326,8 @@
         def _():
             part_in[col] = part_out[step]
 
+    for one in loads[3:6]:
+        one.wait()
     gate = jax.nn.sigmoid(matmul(normed.astype(jnp.bfloat16), out_gate[...]))
     for sender in range(n_col):
 
@@ -323,6 +343,8 @@
     after = (pair_ref[...].astype(jnp.float32) + gate * change).astype(jnp.bfloat16)
     after = after.astype(jnp.float32)
 
+    for one in loads[6:]:
+        one.wait()
     normed = norm_rows(after, inc_norm[...]).astype(jnp.bfloat16)
     left_in[col] = masked_half(normed, inc_proj, 0, hidden, mask)
     for step in range(1, n_col):
@@ -390,19 +412,25 @@
     size, _, channels = pair.shape
     tokens = size * size
     rest = [leaf[None, :] if leaf.ndim == 1 else leaf for leaf in rest]
+    operands = [pair.reshape(tokens, channels)] + rest
     vmem = pl.BlockSpec(memory_space=pltpu.VMEM)
+    hbm = pl.BlockSpec(memory_space=pltpu.HBM)
     narrow = pltpu.VMEM((4, tokens, channels), jnp.bfloat16)
     wide = pltpu.VMEM((tokens, channels), jnp.float32)
     result = pl.pallas_call(
         functools.partial(block_kernel, size, n_row, n_col),
         out_shape=jax.ShapeDtypeStruct((tokens, channels), jnp.bfloat16),
-        in_specs=[pl.BlockSpec(memory_space=pltpu.SMEM)] + [vmem] * (1 + len(rest)),
+        in_specs=[pl.BlockSpec(memory_space=pltpu.SMEM)] + [hbm] * len(operands),
         out_specs=vmem,
-        scratch_shapes=[wide] * 4 + [narrow] * 6 + [pltpu.SemaphoreType.DMA((4,))] * 8,
+        scratch_shapes=[pltpu.VMEM(leaf.shape, leaf.dtype) for leaf in operands]
+        + [wide] * 4
+        + [narrow] * 6
+        + [pltpu.SemaphoreType.DMA((4,))] * 8
+        + [pltpu.SemaphoreType.DMA((len(operands),))],
         compiler_params=pltpu.CompilerParams(
-            collective_id=0, has_side_effects=True, vmem_limit_bytes=48 * 1024 * 1024
+            collective_id=0, has_side_effects=True, vmem_limit_bytes=62 * 1024 * 1024
         ),
-    )(residue_count, pair.reshape(tokens, channels), *rest)
+    )(residue_count, *operands)
     return result.reshape(size, size, channels)
 
 

time: 60.3 us -> 53.7 us (0.89)
  local copies, waits for them, and re-layouts: 8.94 us -> 1.59 us
  Pallas kernels: 50.1 us -> 51.3 us
    unnamed x29 -> x1, local copies, waits for them, and re-layouts: 8.94 us -> 1.59 us
    pallas_call x1, Pallas kernels: 50.1 us -> 51.3 us  [local_kernel(): pl.pallas_call(functools.partial(block_kernel, size, n_row, n_col), out_s...]
where the time goes in v2:
time: 53.7 us; the launch traced here: 53.5 us
  Pallas kernels  51.3 us (96%)
  local copies, waits for them, and re-layouts  1.59 us (3%)
  between operations  0.66 us (1%)
    pallas_call x1, Pallas kernels, local_kernel(): pl.pallas_call(functools.partial(block_kernel, size, n_row, n_col), out_s...  51.3 us
    unnamed x1, local copies, waits for them, and re-layouts  1.59 us

profile of v2, /device:TPU:27, one launch (start us, length us, event | category | flops | bytes accessed | tf_op | source)
XLA Modules:
  0.0 53.5 jit_solution(2526765030356234556)
XLA Ops:
  0.7 51.3 %shard_map.145 = bf16[576,128]{1,0:T(8,128)(2,1)} custom-call(s32[1]{0:T(128)S(6)} %copy.17.count_ref, bf16[576,128]{1,0:T(8,128)(2,1)} %bitcast.8, f32[1,128]{1,0:T(1,128)} %bitcast.9, bf16[128,512]{1,0:T(8,128)(2,1)} %refs_2_.1, bf16[128,128]{1,0:T(8,128)(2,1)} %refs_3_.1, f32[1,128]{1,0:T(1,128)} %bitcast.10, bf16[128,128]{1,0:T(8,128)(2,1)} %refs_5_.1, ...), custom_call_target="tpu_custom_call" | custom-call | tf_op jit(solution)/shard_map/pallas_call | solution.py:420
  51.9 1.6 %copy.18 = bf16[24,24,128]{2,1,0:T(8,128)(2,1)} copy(bf16[24,24,128]{2,1,0:T(8,128)(2,1)} %bitcast.7) | data formatting | bytes 294912

commit v3 on v2

--- a/solution.py
+++ b/solution.py
@@ -141,22 +141,28 @@
     return (mask * jax.nn.sigmoid(part[:, :hidden]) * part[:, hidden:]).astype(jnp.bfloat16)
 
 
-def contract(size, left_ref, right_ref, out_ref, out_slot):
-    for first in range(0, size, 8):
-
-        def step(k, totals, first=first):
-            base = pl.multiple_of(k * size, 8)
-            block = right_ref[pl.ds(base, size), :]
-            return tuple(
-                total + left_ref[pl.ds(base + first + place, 1), :] * block
-                for place, total in enumerate(totals)
-            )
-
-        zero = jnp.zeros((size, right_ref.shape[1]), jnp.float32)
-        totals = lax.fori_loop(0, size, step, (zero,) * 8, unroll=2)
-        out_ref[out_slot, first * size : (first + 8) * size, :] = jnp.concatenate(
-            totals, axis=0
-        ).astype(jnp.bfloat16)
+def contract(size, left_ref, right_ref, out_ref, out_slot, piece):
+    def step(k, totals):
+        block = right_ref[pl.ds(pl.multiple_of(k * size, 8), size), :]
+        base = pl.multiple_of((piece * size + k) * 8, 8)
+        return tuple(
+            total + left_ref[pl.ds(base + place, 1), :] * block
+            for place, total in enumerate(totals)
+        )
+
+    zero = jnp.zeros((size, right_ref.shape[1]), jnp.float32)
+    totals = lax.fori_loop(0, size, step, (zero,) * 8, unroll=2)
+    out_ref[out_slot, piece * 8 * size : (piece + 1) * 8 * size, :] = jnp.concatenate(
+        totals, axis=0
+    ).astype(jnp.bfloat16)
+
+
+def by_pieces(size, values, out_ref):
+    for k in range(size):
+        for piece in range(size // 8):
+            source = k * size + piece * 8
+            target = (piece * size + k) * 8
+            out_ref[target : target + 8, :] = values[source : source + 8, :]
 
 
 def block_kernel(
@@ -207,6 +213,7 @@
     row = lax.axis_index("row")
     col = lax.axis_index("col")
     tokens = size * size
+    pieces = range(size // 8)
     hidden = out_proj.shape[1] // 4
 
     loads = [
@@ -250,39 +257,45 @@
             {"row": row_peer(hop)},
         )
 
-    def to_owner(step):
-        return copy(
-            part_out.at[step], part_in.at[col], send_b.at[step], recv_b.at[col],
+    def to_owner(step, piece):
+        part = pl.ds(piece * 8 * size, 8 * size)
+        return copy(
+            part_out.at[step, part], part_in.at[col, part], send_b.at[step, piece], recv_b.at[col, piece],
             {"col": row_peer(step)},
         )
 
-    def from_col(sender):
-        return copy(
-            part_out.at[0], part_in.at[sender], send_b.at[0], recv_b.at[sender],
+    def from_col(sender, piece):
+        part = pl.ds(piece * 8 * size, 8 * size)
+        return copy(
+            part_out.at[0, part], part_in.at[sender, part], send_b.at[0, piece], recv_b.at[sender, piece],
             {"col": sender},
         )
 
-    def to_col(step):
-        return copy(
-            left_in.at[col], left_in.at[col], send_c.at[step], recv_c.at[col],
+    def to_col(step, piece):
+        part = pl.ds(piece * 8 * size, 8 * size)
+        return copy(
+            left_in.at[col, part], left_in.at[col, part], send_c.at[step, piece], recv_c.at[col, piece],
             {"col": col_peer(step)},
         )
 
-    def left_from(sender):
-        return copy(
-            left_in.at[col], left_in.at[sender], send_c.at[0], recv_c.at[sender],
+    def left_from(sender, piece):
+        part = pl.ds(piece * 8 * size, 8 * size)
+        return copy(
+            left_in.at[col, part], left_in.at[sender, part], send_c.at[0, piece], recv_c.at[sender, piece],
             {"col": sender},
         )
 
-    def to_row_owner(step):
-        return copy(
-            sum_out.at[step], sum_in.at[row], send_d.at[step], recv_d.at[row],
+    def to_row_owner(step, piece):
+        part = pl.ds(piece * 8 * size, 8 * size)
+        return copy(
+            sum_out.at[step, part], sum_in.at[row, part], send_d.at[step, piece], recv_d.at[row, piece],
             {"row": col_peer(step)},
         )
 
-    def from_row(sender):
-        return copy(
-            sum_out.at[0], sum_in.at[sender], send_d.at[0], recv_d.at[sender],
+    def from_row(sender, piece):
+        part = pl.ds(piece * 8 * size, 8 * size)
+        return copy(
+            sum_out.at[0, part], sum_in.at[sender, part], send_d.at[0, piece], recv_d.at[sender, piece],
             {"row": sender},
         )
 
@@ -309,18 +322,20 @@
     pl.semaphore_wait(barrier, n_row + n_col - 2)
     for step in (2, 1):
         to_row(step).start()
-    wide_left[...] = masked_half(turned, out_proj, 0, hidden, mask_turned).astype(jnp.float32)
+    left = masked_half(turned, out_proj, 0, hidden, mask_turned)
+    by_pieces(size, left.astype(jnp.float32), wide_left)
     for step in range(n_row):
         if step > 0:
             to_row(step).wait_recv()
         if step == 2:
             to_row(3).start()
         wide_right[...] = right_in[step].astype(jnp.float32)
-        contract(size, wide_left, wide_right, part_out, step)
-
-        @pl.when(row_peer(step) != col)
-        def _():
-            to_owner(step).start()
+        for piece in pieces:
+            contract(size, wide_left, wide_right, part_out, step, piece)
+
+            @pl.when(row_peer(step) != col)
+            def _():
+                to_owner(step, piece).start()
 
         @pl.when(row_peer(step) == col)
         def _():
@@ -333,7 +348,8 @@
 
         @pl.when(sender != col)
         def _():
-            from_col(sender).wait_recv()
+            for piece in pieces:
+                from_col(sender, piece).wait_recv()
 
     mixed = part_in[0].astype(jnp.float32)
     for sender in range(1, n_col):
@@ -346,33 +362,41 @@
     for one in loads[6:]:
         one.wait()
     normed = norm_rows(after, inc_norm[...]).astype(jnp.bfloat16)
-    left_in[col] = masked_half(normed, inc_proj, 0, hidden, mask)
-    for step in range(1, n_col):
-        to_col(step).start()
+    left = masked_half(normed, inc_proj, 0, hidden, mask)
+    by_pieces(size, left.astype(jnp.float32), wide_left)
+    left_in[col] = wide_left[...].astype(jnp.bfloat16)
+    for piece in pieces:
+        for step in (2, 1, 3):
+            to_col(step, piece).start()
     wide_right[...] = masked_half(normed, inc_proj, 2 * hidden, hidden, mask).astype(jnp.float32)
     gate = jax.nn.sigmoid(matmul(normed, inc_gate[...]))
     turn_a[...] = after
     turn_b[...] = gate
-    for step in (0, 1, 3, 2):
+    order = [(0, piece) for piece in pieces]
+    order += [(step, piece) for piece in pieces for step in (1, 3, 2)]
+    for step, piece in order:
         owner = col_peer(step)
         if step > 0:
-            left_from(owner).wait_recv()
-        wide_left[...] = left_in[owner].astype(jnp.float32)
-        contract(size, wide_left, wide_right, sum_out, step)
+            left_from(owner, piece).wait_recv()
+            part = pl.ds(piece * 8 * size, 8 * size)
+            wide_left[part, :] = left_in[owner, part, :].astype(jnp.float32)
+        contract(size, wide_left, wide_right, sum_out, step, piece)
 
         @pl.when(owner != row)
         def _():
-            to_row_owner(step).start()
+            to_row_owner(step, piece).start()
 
         @pl.when(owner == row)
         def _():
-            sum_in[row] = sum_out[step]
+            part = pl.ds(piece * 8 * size, 8 * size)
+            sum_in[row, part, :] = sum_out[step, part, :]
 
     for sender in range(n_row):
 
         @pl.when(sender != row)
         def _():
-            from_row(sender).wait_recv()
+            for piece in pieces:
+                from_row(sender, piece).wait_recv()
 
     mixed = sum_in[0].astype(jnp.float32)
     for sender in range(1, n_row):
@@ -397,15 +421,18 @@
 
         @pl.when(row_peer(step) != col)
         def _():
-            to_owner(step).wait_send()
+            for piece in pieces:
+                to_owner(step, piece).wait_send()
 
     for step in range(1, n_col):
-        to_col(step).wait_send()
+        for piece in pieces:
+            to_col(step, piece).wait_send()
     for step in range(n_col):
 
         @pl.when(col_peer(step) != row)
         def _():
-            to_row_owner(step).wait_send()
+            for piece in pieces:
+                to_row_owner(step, piece).wait_send()
 
 
 def local_kernel(n_row, n_col, pair, residue_count, *rest):
@@ -425,7 +452,8 @@
         scratch_shapes=[pltpu.VMEM(leaf.shape, leaf.dtype) for leaf in operands]
         + [wide] * 4
         + [narrow] * 6
-        + [pltpu.SemaphoreType.DMA((4,))] * 8
+        + [pltpu.SemaphoreType.DMA((4,))] * 2
+        + [pltpu.SemaphoreType.DMA((4, size // 8))] * 6
         + [pltpu.SemaphoreType.DMA((len(operands),))],
         compiler_params=pltpu.CompilerParams(
             collective_id=0, has_side_effects=True, vmem_limit_bytes=62 * 1024 * 1024

time: 53.7 us -> 48.3 us (0.90)
  the two profiles are of different devices: /device:TPU:27 before, /device:TPU:18 now
where the time goes in v3:
time: 48.3 us; the launch traced here: 48.1 us
  Pallas kernels  45.9 us (95%)
  local copies, waits for them, and re-layouts  1.59 us (3%)
  between operations  0.66 us (1%)
    pallas_call x1, Pallas kernels, local_kernel(): pl.pallas_call(functools.partial(block_kernel, size, n_row, n_col), out_s...  45.9 us
    unnamed x1, local copies, waits for them, and re-layouts  1.59 us

profile of v3, /device:TPU:18, one launch (start us, length us, event | category | flops | bytes accessed | tf_op | source)
XLA Modules:
  0.0 48.1 jit_solution(3613401985132381138)
XLA Ops:
  0.7 45.9 %shard_map.145 = bf16[576,128]{1,0:T(8,128)(2,1)} custom-call(s32[1]{0:T(128)S(6)} %copy.17.count_ref, bf16[576,128]{1,0:T(8,128)(2,1)} %bitcast.8, f32[1,128]{1,0:T(1,128)} %bitcast.9, bf16[128,512]{1,0:T(8,128)(2,1)} %refs_2_.1, bf16[128,128]{1,0:T(8,128)(2,1)} %refs_3_.1, f32[1,128]{1,0:T(1,128)} %bitcast.10, bf16[128,128]{1,0:T(8,128)(2,1)} %refs_5_.1, ...), custom_call_target="tpu_custom_call" | custom-call | tf_op jit(solution)/shard_map/pallas_call | solution.py:447
  46.5 1.6 %copy.18 = bf16[24,24,128]{2,1,0:T(8,128)(2,1)} copy(bf16[24,24,128]{2,1,0:T(8,128)(2,1)} %bitcast.7) | data formatting | bytes 294912

commit v4 on v3

--- a/solution.py
+++ b/solution.py
@@ -151,7 +151,7 @@
         )
 
     zero = jnp.zeros((size, right_ref.shape[1]), jnp.float32)
-    totals = lax.fori_loop(0, size, step, (zero,) * 8, unroll=2)
+    totals = lax.fori_loop(0, size, step, (zero,) * 8, unroll=6)
     out_ref[out_slot, piece * 8 * size : (piece + 1) * 8 * size, :] = jnp.concatenate(
         totals, axis=0
     ).astype(jnp.bfloat16)
@@ -366,7 +366,7 @@
     by_pieces(size, left.astype(jnp.float32), wide_left)
     left_in[col] = wide_left[...].astype(jnp.bfloat16)
     for piece in pieces:
-        for step in (2, 1, 3):
+        for step in (1, 3, 2):
             to_col(step, piece).start()
     wide_right[...] = masked_half(normed, inc_proj, 2 * hidden, hidden, mask).astype(jnp.float32)
     gate = jax.nn.sigmoid(matmul(normed, inc_gate[...]))

time: 48.3 us -> 47.3 us (0.979)
  the two profiles are of different devices: /device:TPU:18 before, /device:TPU:27 now
where the time goes in v4:
time: 47.3 us; the launch traced here: 47.1 us
  Pallas kernels  44.8 us (95%)
  local copies, waits for them, and re-layouts  1.59 us (3%)
  between operations  0.66 us (1%)
    pallas_call x1, Pallas kernels, local_kernel(): pl.pallas_call(functools.partial(block_kernel, size, n_row, n_col), out_s...  44.8 us
    unnamed x1, local copies, waits for them, and re-layouts  1.59 us

profile of v4, /device:TPU:27, one launch (start us, length us, event | category | flops | bytes accessed | tf_op | source)
XLA Modules:
  0.0 47.1 jit_solution(9924421167905236492)
XLA Ops:
  0.7 44.8 %shard_map.145 = bf16[576,128]{1,0:T(8,128)(2,1)} custom-call(s32[1]{0:T(128)S(6)} %copy.17.count_ref, bf16[576,128]{1,0:T(8,128)(2,1)} %bitcast.8, f32[1,128]{1,0:T(1,128)} %bitcast.9, bf16[128,512]{1,0:T(8,128)(2,1)} %refs_2_.1, bf16[128,128]{1,0:T(8,128)(2,1)} %refs_3_.1, f32[1,128]{1,0:T(1,128)} %bitcast.10, bf16[128,128]{1,0:T(8,128)(2,1)} %refs_5_.1, ...), custom_call_target="tpu_custom_call" | custom-call | tf_op jit(solution)/shard_map/pallas_call | solution.py:447
  45.5 1.6 %copy.18 = bf16[24,24,128]{2,1,0:T(8,128)(2,1)} copy(bf16[24,24,128]{2,1,0:T(8,128)(2,1)} %bitcast.7) | data formatting | bytes 294912
